TPU v7x, 32 devices: a whole 2x2x4 slice. The times are simulated.
32 devices in a mesh: req: 4 (over y, x), head: 8 (over z, core).
Axes of the slice: x: 2, y: 2, z: 4, core: 2. Of those that a mesh axis runs over, the one named last changes fastest.
Arguments:
- hidden_in: bfloat16 [2048, 2048], P(('req', 'head')), may hold values from -6 to 6
- queries: bfloat16 [2048, 2048], P(('req', 'head')), may hold values from -160 to 160
- keys_values: bfloat16 [2048, 1024], P(('req', 'head')), may hold values from -10 to 10
- request_of_row: int32 [2048], P('req'), may hold values from 0 to 7, as said below
- page_route: int32 [4, 8, 4], P('req', 'head'), may hold values from 0 to 3, each once within a row
- expert_ids: int32 [2048, 6], P(('req', 'head')), may hold values from 0 to 31, all different within a row; in each aligned block of 64 rows (0 to 63, 64 to 127, ...) at most 14 rows name the same one
- expert_weights: float32 [2048, 6], P(('req', 'head')), may hold values from 0.05 to 0.5
- norm_gain: float32 [2048], replicated, may hold values from 0.25 to 1.75
- shared_gate_up: bfloat16 [2048, 2, 1408], replicated, may hold values from -0.125 to 0.125
- shared_down: bfloat16 [1408, 2048], replicated, may hold values from -0.15625 to 0.15625
- expert_gate_up: bfloat16 [32, 2, 1408, 2048], P('head', None, 'req'), may hold values from -0.125 to 0.125
- expert_down: bfloat16 [32, 1408, 2048], P('head', 'req'), may hold values from -0.15625 to 0.15625
Outputs:
- layer_out: bfloat16 [2048, 2048], P(('req', 'head'))
Inputs may be any that keep to these rules, and one draw needn't show every extreme that they name: `request_of_row`: each group of 512 rows g holds two requests, ids 2 g then 2 g + 1, each a whole number of pages of 16 rows and at least 32 rows long. `page_route`: for every device, the groups receiving its pages form a permutation of all groups. `expert_ids`: each row names 6 different experts; among the rows of one device no expert is named more than 14 times, and some device names some expert exactly 14 times.
All inputs are finite; a program needn't handle non-finite values.
Results may differ from a plain program's by a relative error of at most 0.006.
Values may be sent and summed in bfloat16 or wider, within the bound.
A program may use at most 192 MiB of HBM per device.

v0:
```python
import jax
import jax.numpy as jnp
from jax import lax
from jax.sharding import PartitionSpec as P

QUERY_HEADS = 16
KEY_VALUE_HEADS = 4
HEAD_SIZE = 128
EXPERTS = 32
TOP = 6
CAP = 14


negative_large = -1e30


def silu_mul(gate_value, upward):
    return gate_value / (1.0 + jnp.exp(-gate_value)) * upward


def expand_rows(arrived_block, gate_up):
    both_parts = jnp.einsum(
        "rhjcd,jkfd->rhjckf", arrived_block, gate_up, preferred_element_type=jnp.float32
    )
    return silu_mul(both_parts[..., 0, :], both_parts[..., 1, :]).astype(jnp.bfloat16)


def project_down(hidden, down_matrix):
    return jnp.einsum("rhjcf,jfd->rhjcd", hidden, down_matrix, preferred_element_type=jnp.float32)


def body(
    hidden_in,
    queries,
    keys_values,
    request_of_row,
    page_route,
    expert_ids,
    expert_weights,
    norm_gain,
    shared_gate_up,
    shared_down,
    expert_gate_up,
    expert_down,
):
    groups = lax.axis_size("req")
    columns = lax.axis_size("head")
    token_rows = hidden_in.shape[0]
    model_width = hidden_in.shape[1]
    page_rows = token_rows // groups
    group_ids = jnp.arange(groups, dtype=jnp.int32)
    page_dest = page_route.reshape(groups)
    matches = (page_dest[None, :] == group_ids[:, None]).astype(jnp.int32)
    dest_order = jnp.sum(matches * group_ids[None, :], axis=1)

    def by_dest(array_in):
        return jnp.take(array_in.reshape(groups, page_rows, array_in.shape[1]), dest_order, axis=0)

    moved_rows = (
        lax.all_to_all(by_dest(hidden_in), "req", split_axis=0, concat_axis=0, tiled=True),
        lax.all_to_all(by_dest(queries), "req", split_axis=0, concat_axis=0, tiled=True),
        lax.all_to_all(by_dest(keys_values), "req", split_axis=0, concat_axis=0, tiled=True),
    )
    resid = moved_rows[0].reshape(token_rows, model_width)
    rows_of_queries = moved_rows[1].reshape(token_rows, QUERY_HEADS * HEAD_SIZE)
    key_value_rows = moved_rows[2].reshape(token_rows, 2 * KEY_VALUE_HEADS * HEAD_SIZE)
    group_fraction = QUERY_HEADS // KEY_VALUE_HEADS
    key_value_width = KEY_VALUE_HEADS * HEAD_SIZE
    score_scale = HEAD_SIZE ** (-0.5)
    query_start = lax.axis_index("head") * token_rows
    segment_query = lax.dynamic_slice_in_dim(request_of_row, query_start, token_rows)
    position_query = query_start + jnp.arange(token_rows, dtype=jnp.int32)
    query_fourfold = rows_of_queries.reshape(token_rows, KEY_VALUE_HEADS, group_fraction, HEAD_SIZE)
    start_state = (
        jnp.full((KEY_VALUE_HEADS, group_fraction, token_rows), negative_large, jnp.float32),
        jnp.zeros((KEY_VALUE_HEADS, group_fraction, token_rows), jnp.float32),
        jnp.zeros((KEY_VALUE_HEADS, group_fraction, token_rows, HEAD_SIZE), jnp.float32),
    )
    kv_piece = lax.all_gather(key_value_rows, "head", axis=0, tiled=True)
    piece_rows = kv_piece.shape[0]
    rows_per_block = 512

    def one_block(block_index, carried_block):
        offset = block_index * rows_per_block
        current_block = lax.dynamic_slice_in_dim(kv_piece, offset, rows_per_block)
        block_keys = current_block[:, :key_value_width].reshape(
            rows_per_block, KEY_VALUE_HEADS, HEAD_SIZE
        )
        block_values = current_block[:, key_value_width:].reshape(
            rows_per_block, KEY_VALUE_HEADS, HEAD_SIZE
        )
        segment_key = lax.dynamic_slice_in_dim(request_of_row, offset, rows_per_block)
        position_key = offset + jnp.arange(rows_per_block, dtype=jnp.int32)
        allowed = (segment_query[:, None] == segment_key[None, :]) & (
            position_key[None, :] <= position_query[:, None]
        )
        running_max, running_sum, accumulated = carried_block
        score = (
            jnp.einsum(
                "tgqd,sgd->gqts", query_fourfold, block_keys, preferred_element_type=jnp.float32
            )
            * score_scale
        )
        masked = jnp.where(allowed, score, negative_large)
        new_max = jnp.maximum(running_max, jnp.max(masked, axis=-1))
        weights = jnp.where(allowed, jnp.exp(masked - new_max[..., None]), 0.0)
        factor = jnp.exp(running_max - new_max)
        running_sum = running_sum * factor + jnp.sum(weights, axis=-1)
        accumulated = accumulated * factor[..., None] + jnp.einsum(
            "gqts,sgd->gqtd",
            weights.astype(jnp.bfloat16),
            block_values,
            preferred_element_type=jnp.float32,
        )
        return (new_max, running_sum, accumulated)

    running_max, running_sum, accumulated = lax.fori_loop(
        0, piece_rows // rows_per_block, one_block, start_state
    )
    context = jnp.transpose(accumulated / running_sum[..., None], (2, 0, 1, 3)).reshape(
        token_rows, QUERY_HEADS * HEAD_SIZE
    )
    mixed_rows = resid.astype(jnp.float32) + context
    mean_square = jnp.mean(mixed_rows * mixed_rows, axis=1, keepdims=True)
    normed = (mixed_rows * lax.rsqrt(mean_square + 1e-06) * norm_gain).astype(jnp.bfloat16)
    pair_expert = expert_ids.reshape(-1)
    hit_table = (pair_expert[:, None] == jnp.arange(EXPERTS, dtype=jnp.int32)[None, :]).astype(
        jnp.int32
    )
    ranks = jnp.sum((jnp.cumsum(hit_table, axis=0) - 1) * hit_table, axis=1)
    slot_of = pair_expert * CAP + ranks
    slots_all = EXPERTS * CAP
    placing = jnp.arange(slots_all, dtype=jnp.int32)[:, None] == slot_of[None, :]
    placing = jnp.any(placing.reshape(slots_all, token_rows, TOP), axis=2).astype(jnp.bfloat16)
    outgoing = jnp.dot(placing, normed, preferred_element_type=jnp.float32).astype(jnp.bfloat16)
    local_experts = expert_gate_up.shape[0]
    outgoing = outgoing.reshape(columns, local_experts * CAP, model_width)
    shared_both = jnp.dot(
        normed, shared_gate_up.reshape(model_width, -1), preferred_element_type=jnp.float32
    ).reshape(token_rows, 2, -1)
    shared_hidden = silu_mul(shared_both[:, 0], shared_both[:, 1]).astype(jnp.bfloat16)
    shared_out = jnp.dot(shared_hidden, shared_down, preferred_element_type=jnp.float32)
    copies = jnp.broadcast_to(outgoing[None], (groups,) + outgoing.shape).reshape(
        groups * columns, local_experts * CAP, model_width
    )
    arrived = lax.all_to_all(copies, ("req", "head"), split_axis=0, concat_axis=0, tiled=True)
    arrived = arrived.reshape(groups, columns, local_experts, CAP, model_width)

    def per_group(arrived_group):
        hidden = expand_rows(arrived_group[None], expert_gate_up)
        return project_down(hidden, expert_down)[0].astype(jnp.bfloat16)

    partial_out = lax.map(per_group, arrived)
    returned = lax.all_to_all(
        partial_out.reshape(groups * columns, local_experts * CAP, model_width),
        ("req", "head"),
        split_axis=0,
        concat_axis=0,
        tiled=True,
    )
    summed = jnp.sum(returned.reshape(groups, slots_all, model_width).astype(jnp.float32), axis=0)
    pair_rows = jnp.take(summed, slot_of, axis=0).reshape(token_rows, TOP, model_width)
    routed = jnp.sum(pair_rows * expert_weights[:, :, None], axis=1)
    return (mixed_rows + shared_out + routed).astype(jnp.bfloat16)


def solution(mesh):
    return jax.shard_map(
        body,
        mesh=mesh,
        in_specs=(
            P(("req", "head"), None),
            P(("req", "head"), None),
            P(("req", "head"), None),
            P("req"),
            P("req", "head", None),
            P(("req", "head"), None),
            P(("req", "head"), None),
            P(),
            P(),
            P(),
            P("head", None, "req", None),
            P("head", "req", None),
        ),
        out_specs=P(("req", "head"), None),
        check_vma=False,
    )
```

profile of v0, /device:TPU:0, one launch (start us, length us, event | category | flops | bytes accessed | tf_op | source)
XLA Modules:
  0.0 489.7 jit_solution(601382824886525123)
XLA Ops:
  6.5 0.8 select_reduce_fusion
  7.4 1.5 gather_fusion
  8.9 10.1 %all_to_all.25 = bf16[4,16,1024]{2,1,0:T(8,128)(2,1)} all-to-all(bf16[4,16,1024]{2,1,0:T(8,128)(2,1)S(1)} %broadcast_select_fusion.2), channel_id=1, replica_groups=mesh['req'=4,'head'=8] {'req'}, dimensions={0} | all-to-all | bytes 262144 | tf_op jit(solution)/shard_map/all_to_all | solution.py:62
  19.1 0.6 gather_fusion.3
  19.7 1.5 gather_fusion.2
  21.2 0.9 broadcast_select_fusion.1
  22.1 3.4 all-to-all-start.2
  25.6 0.1 eq.82
  25.8 0.1 reshape.223
  25.9 0.9 reduce-window.6
  26.8 0.2 slice_reduce_fusion
  27.5 0.2 fusion.30
  27.7 3.2 all-to-all-done.2
  30.9 3.4 all-to-all-start
  34.4 0.2 reshape_reshape.3
  34.6 5.1 %all-to-all-done = bf16[4,16,2048]{2,1,0:T(8,128)(2,1)S(1)} async-done(((bf16[4,16,2048]{2,1,0:T(8,128)(2,1)}), bf16[4,16,2048]{2,1,0:T(8,128)(2,1)S(1)}, u32[]{:S(2)}, u32[]{:S(2)}) %all-to-all-start) | async-done | bytes 262176 | tf_op jit(solution)/shard_map/all_to_all | solution.py:60
  39.6 0.4 reshape.229
  40.0 1.0 all-gather.2.cloned.1.call-done
  41.1 1.3 fusion.51
  42.3 0.2 copy.93
  42.6 0.2 copy.96
  42.8 0.5 fusion.20
  43.3 0.7 fusion.21
  44.1 1.0 multiply_reduce_fusion.1
  45.1 0.3 copy.98
  45.4 0.2 reshape.221
  45.7 0.8 copy-done.2
  46.5 0.7 convolution_convert_fusion
  47.2 3.9 broadcast_in_dim.95
  51.1 4.5 all-to-all-start.3
  55.6 162.3 %all-to-all-done.3 = bf16[32,56,2048]{2,1,0:T(8,128)(2,1)} async-done(((bf16[32,56,2048]{2,1,0:T(8,128)(2,1)}), bf16[32,56,2048]{2,1,0:T(8,128)(2,1)}, u32[]{:S(2)}, u32[]{:S(2)}) %all-to-all-start.3) | async-done | bytes 7340064 | tf_op jit(solution)/shard_map/all_to_all | solution.py:146
  217.8 10.1 %copy.107 = bf16[32,56,2048]{2,0,1:T(8,128)(2,1)} copy(bf16[32,56,2048]{2,1,0:T(8,128)(2,1)} %all-to-all-done.3) | data formatting | bytes 14680064 | tf_op jit(solution)/shard_map/all_to_all | solution.py:146
  227.9 54.3 %while.2 = (s32[]{:T(128)}, bf16[4,8,4,14,2048]{4,1,0,3,2:T(8,128)(2,1)}, bf16[4,8,4,14,2048]{4,1,0,3,2:T(8,128)(2,1)}, bf16[4,2,352,2048]{3,2,1,0:T(8,128)(2,1)}, bf16[4,352,2048]{2,1,0:T(8,128)(2,1)}, /*index=5*/s32[]{:T(128)}) while((s32[]{:T(128)}, bf16[4,8,4,14,2048]{4,1,0,3,2:T(8,128)(2,1)}, bf16[4,8,4,14,2048]{4,1,0,3,2:T(8,128)(2,1)}, ...), condition=%wide.region_9.11_spmd, body=%wide.region_8.10_spmd.sunk | while | flops 1939474432 | bytes 48136324 | solution.py:153
  227.9 1.8 constant_dynamic-slice_fusion.2
  229.7 8.3 %fusion.67 = f32[1,8,4,14,2,352]{5,3,4,1,2,0:T(8,128)S(1)} fusion(bf16[4,2,352,2048]{3,2,1,0:T(8,128)(2,1)} %get-tuple-element.157, bf16[1,8,4,14,2048]{4,1,0,3,2:T(8,128)(2,1)S(1)} %constant_dynamic-slice_fusion.2), kind=kOutput, calls=%fused_computation.12.clone.1 | convolution fusion | flops 1291845632 | bytes 14630912 | tf_op jit(solution)/shard_map/while/body/eval_jaxpr/rhjcd,jkfd->rhjckf/dot_general | solution.py:22
  238.0 1.3 fusion.68
  239.3 2.2 copy_dynamic-update-slice_fusion.2
  241.5 1.8 constant_dynamic-slice_fusion.2
  243.3 8.3 %fusion.67 = f32[1,8,4,14,2,352]{5,3,4,1,2,0:T(8,128)S(1)} fusion(bf16[4,2,352,2048]{3,2,1,0:T(8,128)(2,1)} %get-tuple-element.157, bf16[1,8,4,14,2048]{4,1,0,3,2:T(8,128)(2,1)S(1)} %constant_dynamic-slice_fusion.2), kind=kOutput, calls=%fused_computation.12.clone.1 | convolution fusion | flops 1291845632 | bytes 14630912 | tf_op jit(solution)/shard_map/while/body/eval_jaxpr/rhjcd,jkfd->rhjckf/dot_general | solution.py:22
  251.6 1.3 fusion.68
  252.9 2.2 copy_dynamic-update-slice_fusion.2
  255.1 1.8 constant_dynamic-slice_fusion.2
  256.9 8.3 %fusion.67 = f32[1,8,4,14,2,352]{5,3,4,1,2,0:T(8,128)S(1)} fusion(bf16[4,2,352,2048]{3,2,1,0:T(8,128)(2,1)} %get-tuple-element.157, bf16[1,8,4,14,2048]{4,1,0,3,2:T(8,128)(2,1)S(1)} %constant_dynamic-slice_fusion.2), kind=kOutput, calls=%fused_computation.12.clone.1 | convolution fusion | flops 1291845632 | bytes 14630912 | tf_op jit(solution)/shard_map/while/body/eval_jaxpr/rhjcd,jkfd->rhjckf/dot_general | solution.py:22
  265.2 1.3 fusion.68
  266.4 2.2 copy_dynamic-update-slice_fusion.2
  268.7 1.8 constant_dynamic-slice_fusion.2
  270.5 8.2 %fusion.67 = f32[1,8,4,14,2,352]{5,3,4,1,2,0:T(8,128)S(1)} fusion(bf16[4,2,352,2048]{3,2,1,0:T(8,128)(2,1)} %get-tuple-element.157, bf16[1,8,4,14,2048]{4,1,0,3,2:T(8,128)(2,1)S(1)} %constant_dynamic-slice_fusion.2), kind=kOutput, calls=%fused_computation.12.clone.1 | convolution fusion | flops 1291845632 | bytes 14630912 | tf_op jit(solution)/shard_map/while/body/eval_jaxpr/rhjcd,jkfd->rhjckf/dot_general | solution.py:22
  278.7 1.3 fusion.68
  280.0 2.2 copy_dynamic-update-slice_fusion.2
  282.3 10.1 %copy.110 = bf16[32,56,2048]{2,1,0:T(8,128)(2,1)} copy(bf16[32,56,2048]{2,0,1:T(8,128)(2,1)} %bitcast.166) | data formatting | bytes 14680064 | tf_op jit(solution)/shard_map/reshape | solution.py:155
  292.4 4.0 all-to-all-start.4
  296.5 0.1 mul.141
  296.9 11.3 %copy.127 = bf16[256,8,2,1408]{3,1,2,0:T(8,128)(2,1)} copy(bf16[256,8,2,1408]{3,2,1,0:T(2,128)(2,1)} %bitcast.165) | data formatting | bytes 23068672
  308.1 15.1 %copy.101 = bf16[2816,2048]{1,0:T(8,128)(2,1)} copy(bf16[2816,2048]{0,1:T(8,128)(2,1)} %bitcast.162) | data formatting | bytes 23068672 | tf_op jit(solution)/shard_map/dot_general | solution.py:138
  323.3 0.2 multiply_convert_fusion.1
  323.5 0.2 copy.100
  323.7 0.2 reshape.274
  323.9 8.7 %fusion.52 = f32[64,2,1408]{2,0,1:T(8,128)} fusion(bf16[64,2048,1]{1,0,2:T(8,128)(2,1)S(1)} %reshape.274, bf16[2,1408,2048]{2,1,0:T(8,128)(2,1)} %bitcast.161), kind=kOutput, calls=%fused_computation.92 | convolution fusion | flops 738197504 | bytes 12517376 | tf_op jit(solution)/shard_map/dot_general | solution.py:138
  332.7 126.0 %all-to-all-done.4 = bf16[32,56,2048]{2,1,0:T(8,128)(2,1)} async-done(((bf16[32,56,2048]{2,1,0:T(8,128)(2,1)}), bf16[32,56,2048]{2,1,0:T(8,128)(2,1)}, u32[]{:S(2)}, u32[]{:S(2)}) %all-to-all-start.4) | async-done | bytes 7340064 | tf_op jit(solution)/shard_map/all_to_all | solution.py:154
  458.6 6.8 %convert_reduce_fusion = f32[448,2048]{1,0:T(8,128)} fusion(bf16[4,448,2048]{2,1,0:T(8,128)(2,1)} %bitcast.142), kind=kLoop, calls=%fused_computation.20 | loop fusion | flops 6422528 | bytes 11010048 | tf_op jit(solution)/shard_map/reduce_sum | solution.py:161
  465.4 6.4 %gather_fusion.1 = f32[384,2048]{1,0:T(8,128)S(1)} fusion(f32[448,2048]{1,0:T(8,128)} %convert_reduce_fusion, s32[1024]{0:T(1024)S(1)} %pad_clamp_fusion), kind=kCustom, calls=%fused_computation.3 | custom fusion | bytes 6292992 | tf_op jit(solution)/shard_map/jit(_take)/gather | solution.py:162
  471.8 2.1 gather.15
  474.0 4.4 multiply_reduce_fusion
  478.4 4.5 fusion.19
  (66 shorter events, 1.3 us)
Async XLA Ops:
  6.5 12.6 %copy-start = (bf16[64,2048]{1,0:T(8,128)(2,1)S(1)}, bf16[64,2048]{1,0:T(8,128)(2,1)}, u32[]{:S(2)}) copy-start(bf16[64,2048]{1,0:T(8,128)(2,1)} %param.17) | copy-start | bytes 786436
  6.5 19.0 %copy-start.5 = (s32[64,6]{0,1:T(8,128)S(1)}, s32[64,6]{0,1:T(8,128)}, u32[]{:S(2)}) copy-start(s32[64,6]{0,1:T(8,128)} %param.21) | copy-start | bytes 4612
  6.5 20.9 %copy-start.8 = (s32[512]{0:T(512)S(1)}, s32[512]{0:T(512)}, u32[]{:S(2)}) copy-start(s32[512]{0:T(512)} %param.19) | copy-start | bytes 6148
  6.5 34.5 %all-gather.2.cloned.1.call-start = ((), (), s32[]{:S(2)}) async-start(), calls=%async_computation.5 | async-start | bytes 1179648 | tf_op jit(solution)/shard_map/all_gather | solution.py:79
  22.1 8.8 %all-to-all-start.2 = ((bf16[4,16,2048]{2,1,0:T(8,128)(2,1)}), bf16[4,16,2048]{2,1,0:T(8,128)(2,1)S(1)}, u32[]{:S(2)}, u32[]{:S(2)}) async-start(bf16[4,16,2048]{2,1,0:T(8,128)(2,1)} %get-tuple-element.106), calls=%async_computation.2 | async-start | bytes 524288 | tf_op jit(solution)/shard_map/all_to_all | solution.py:61
  30.9 8.8 %all-to-all-start = ((bf16[4,16,2048]{2,1,0:T(8,128)(2,1)}), bf16[4,16,2048]{2,1,0:T(8,128)(2,1)S(1)}, u32[]{:S(2)}, u32[]{:S(2)}) async-start(bf16[4,16,2048]{2,1,0:T(8,128)(2,1)} %get-tuple-element.105), calls=%async_computation | async-start | bytes 524288 | tf_op jit(solution)/shard_map/all_to_all | solution.py:60
  45.0 1.5 copy-start.6
  45.7 0.8 copy-start.2
  51.1 166.7 %all-to-all-start.3 = ((bf16[32,56,2048]{2,1,0:T(8,128)(2,1)}), bf16[32,56,2048]{2,1,0:T(8,128)(2,1)}, u32[]{:S(2)}, u32[]{:S(2)}) async-start(bf16[32,56,2048]{2,1,0:T(8,128)(2,1)} %bitcast.164), calls=%async_computation.3 | async-start | bytes 14680064 | tf_op jit(solution)/shard_map/all_to_all | solution.py:146
  227.9 10.1 %slice-start = ((s8[5767168]{0:T(1024)(128)(4,1)}), s8[4194304]{0:T(1024)(128)(4,1)S(1)}, s32[]{:S(2)}) async-start(s8[5767168]{0:T(1024)(128)(4,1)} %bitcast.159), calls=%async_computation.6 | async-start | bytes 8388608 | tf_op jit(solution)/shard_map/while
  229.7 8.3 %slice-start.1 = ((s8[5767168]{0:T(1024)(128)(4,1)}), s8[1572864]{0:T(1024)(128)(4,1)S(1)}, s32[]{:S(2)}) async-start(s8[5767168]{0:T(1024)(128)(4,1)} %bitcast.159), calls=%async_computation.7 | async-start | bytes 3145728 | tf_op jit(solution)/shard_map/while
  241.5 10.1 %slice-start = ((s8[5767168]{0:T(1024)(128)(4,1)}), s8[4194304]{0:T(1024)(128)(4,1)S(1)}, s32[]{:S(2)}) async-start(s8[5767168]{0:T(1024)(128)(4,1)} %bitcast.159), calls=%async_computation.6 | async-start | bytes 8388608 | tf_op jit(solution)/shard_map/while
  243.3 8.3 %slice-start.1 = ((s8[5767168]{0:T(1024)(128)(4,1)}), s8[1572864]{0:T(1024)(128)(4,1)S(1)}, s32[]{:S(2)}) async-start(s8[5767168]{0:T(1024)(128)(4,1)} %bitcast.159), calls=%async_computation.7 | async-start | bytes 3145728 | tf_op jit(solution)/shard_map/while
  255.1 10.1 %slice-start = ((s8[5767168]{0:T(1024)(128)(4,1)}), s8[4194304]{0:T(1024)(128)(4,1)S(1)}, s32[]{:S(2)}) async-start(s8[5767168]{0:T(1024)(128)(4,1)} %bitcast.159), calls=%async_computation.6 | async-start | bytes 8388608 | tf_op jit(solution)/shard_map/while
  256.9 8.3 %slice-start.1 = ((s8[5767168]{0:T(1024)(128)(4,1)}), s8[1572864]{0:T(1024)(128)(4,1)S(1)}, s32[]{:S(2)}) async-start(s8[5767168]{0:T(1024)(128)(4,1)} %bitcast.159), calls=%async_computation.7 | async-start | bytes 3145728 | tf_op jit(solution)/shard_map/while
  268.7 10.0 %slice-start = ((s8[5767168]{0:T(1024)(128)(4,1)}), s8[4194304]{0:T(1024)(128)(4,1)S(1)}, s32[]{:S(2)}) async-start(s8[5767168]{0:T(1024)(128)(4,1)} %bitcast.159), calls=%async_computation.6 | async-start | bytes 8388608 | tf_op jit(solution)/shard_map/while
  270.4 8.3 %slice-start.1 = ((s8[5767168]{0:T(1024)(128)(4,1)}), s8[1572864]{0:T(1024)(128)(4,1)S(1)}, s32[]{:S(2)}) async-start(s8[5767168]{0:T(1024)(128)(4,1)} %bitcast.159), calls=%async_computation.7 | async-start | bytes 3145728 | tf_op jit(solution)/shard_map/while
  292.4 4.3 copy-start.7
  292.4 166.2 %all-to-all-start.4 = ((bf16[32,56,2048]{2,1,0:T(8,128)(2,1)}), bf16[32,56,2048]{2,1,0:T(8,128)(2,1)}, u32[]{:S(2)}, u32[]{:S(2)}) async-start(bf16[32,56,2048]{2,1,0:T(8,128)(2,1)} %copy.110), calls=%async_computation.4 | async-start | bytes 14680064 | tf_op jit(solution)/shard_map/all_to_all | solution.py:154
  473.9 4.4 copy-start.3
  473.9 4.5 copy-start.4
  474.0 8.9 %copy-start.1 = (bf16[64,2048]{1,0:T(8,128)(2,1)S(1)}, bf16[64,2048]{1,0:T(8,128)(2,1)}, u32[]{:S(2)}) copy-start(bf16[64,2048]{1,0:T(8,128)(2,1)} %param.17) | copy-start | bytes 786436
Sparse Core Ops, SparseCore 0:
  19.2 21.8 all-gather.1
where the time goes:
time: 491 us; the launch traced here: 490 us
  waiting for transfers between devices  298 us (61%)
  local copies, waits for them, and re-layouts  84 us (17%)
  matrix products  53.5 us (11%)
  other arithmetic  15.4 us (3%)
  starting transfers between devices  15.3 us (3%)
  between operations  13.7 us (3%)
  blocking collectives  10.1 us (2%)
    all_to_all x1, waiting for transfers between devices, body(): lax.all_to_all(copies, ('req', 'head'), split_axis=0, concat_axis=0, tile...  162 us
    all_to_all x1, waiting for transfers between devices, body(): lax.all_to_all(partial_out.reshape(groups * columns, local_experts * CAP,...  126 us
    dot_general x4, matrix products, expand_rows(): jnp.einsum('rhjcd,jkfd->rhjckf', arrived_block, gate_up, preferred_elemen...  33 us
    dot_general x1, local copies, waits for them, and re-layouts, body(): jnp.dot(normed, shared_gate_up.reshape(model_width, -1), preferred_elemen...  15.1 us
    unnamed x21, local copies, waits for them, and re-layouts  12.3 us
    reshape x1, local copies, waits for them, and re-layouts, body(): partial_out.reshape(groups * columns, local_experts * CAP, model_width)  10.1 us
    all_to_all x1, blocking collectives, body(): lax.all_to_all(by_dest(keys_values), 'req', split_axis=0, concat_axis=0,...  10.1 us
    all_to_all x1, local copies, waits for them, and re-layouts, body(): lax.all_to_all(copies, ('req', 'head'), split_axis=0, concat_axis=0, tile...  10.1 us
  transfers between devices with their start and end apart: 5, of which 5 were waited for; matrix products, arithmetic and copies ran while one was open for 9% of the time, Pallas kernels for 0%

commit v1 on v0

--- a/solution.py
+++ b/solution.py
@@ -18,15 +18,31 @@
     return gate_value / (1.0 + jnp.exp(-gate_value)) * upward
 
 
-def expand_rows(arrived_block, gate_up):
-    both_parts = jnp.einsum(
-        "rhjcd,jkfd->rhjckf", arrived_block, gate_up, preferred_element_type=jnp.float32
-    )
-    return silu_mul(both_parts[..., 0, :], both_parts[..., 1, :]).astype(jnp.bfloat16)
-
-
-def project_down(hidden, down_matrix):
-    return jnp.einsum("rhjcf,jfd->rhjcd", hidden, down_matrix, preferred_element_type=jnp.float32)
+def slot_tables(expert_ids, expert_weights, local_experts, token_rows, devices):
+    all_ids = lax.all_gather(expert_ids, ("req", "head"), axis=0, tiled=True)
+    all_weights = lax.all_gather(expert_weights, ("req", "head"), axis=0, tiled=True)
+    first = lax.axis_index("head") * local_experts
+    mine = first + jnp.arange(local_experts, dtype=jnp.int32)
+    hit = all_ids[:, :, None] == mine[None, None, :]
+    pair_weight = jnp.sum(jnp.where(hit, all_weights[:, :, None], 0.0), axis=1)
+    named = jnp.any(hit, axis=1).reshape(devices, token_rows, local_experts)
+    before = jnp.tril(jnp.ones((token_rows, token_rows), jnp.bfloat16), -1)
+    rank = jnp.einsum(
+        "ut,dtj->duj", before, named.astype(jnp.bfloat16), preferred_element_type=jnp.float32
+    ).astype(jnp.int32)
+    joined = 4
+    blocks = devices // joined
+    place = jnp.arange(devices, dtype=jnp.int32)[:, None, None] % joined * CAP + rank
+    place = jnp.where(named, place, -1).reshape(blocks, joined * token_rows, local_experts)
+    place = jnp.transpose(place, (0, 2, 1))
+    slots = jnp.arange(joined * CAP, dtype=jnp.int32)
+    placing = place[:, :, None, :] == slots[None, None, :, None]
+    pair_weight = jnp.transpose(
+        pair_weight.reshape(blocks, joined * token_rows, local_experts), (0, 2, 1)
+    )
+    slot_weight = jnp.sum(jnp.where(placing, pair_weight[:, :, None, :], 0.0), axis=3)
+    slot_weight = jnp.transpose(slot_weight, (1, 0, 2)).reshape(local_experts, -1)
+    return placing.astype(jnp.bfloat16), slot_weight
 
 
 def body(
@@ -123,44 +139,49 @@
     mixed_rows = resid.astype(jnp.float32) + context
     mean_square = jnp.mean(mixed_rows * mixed_rows, axis=1, keepdims=True)
     normed = (mixed_rows * lax.rsqrt(mean_square + 1e-06) * norm_gain).astype(jnp.bfloat16)
-    pair_expert = expert_ids.reshape(-1)
-    hit_table = (pair_expert[:, None] == jnp.arange(EXPERTS, dtype=jnp.int32)[None, :]).astype(
-        jnp.int32
-    )
-    ranks = jnp.sum((jnp.cumsum(hit_table, axis=0) - 1) * hit_table, axis=1)
-    slot_of = pair_expert * CAP + ranks
-    slots_all = EXPERTS * CAP
-    placing = jnp.arange(slots_all, dtype=jnp.int32)[:, None] == slot_of[None, :]
-    placing = jnp.any(placing.reshape(slots_all, token_rows, TOP), axis=2).astype(jnp.bfloat16)
-    outgoing = jnp.dot(placing, normed, preferred_element_type=jnp.float32).astype(jnp.bfloat16)
-    local_experts = expert_gate_up.shape[0]
-    outgoing = outgoing.reshape(columns, local_experts * CAP, model_width)
-    shared_both = jnp.dot(
-        normed, shared_gate_up.reshape(model_width, -1), preferred_element_type=jnp.float32
-    ).reshape(token_rows, 2, -1)
+    shared_both = jnp.einsum(
+        "td,dcf->tcf", normed, shared_gate_up, preferred_element_type=jnp.float32
+    )
     shared_hidden = silu_mul(shared_both[:, 0], shared_both[:, 1]).astype(jnp.bfloat16)
     shared_out = jnp.dot(shared_hidden, shared_down, preferred_element_type=jnp.float32)
-    copies = jnp.broadcast_to(outgoing[None], (groups,) + outgoing.shape).reshape(
-        groups * columns, local_experts * CAP, model_width
-    )
-    arrived = lax.all_to_all(copies, ("req", "head"), split_axis=0, concat_axis=0, tiled=True)
-    arrived = arrived.reshape(groups, columns, local_experts, CAP, model_width)
-
-    def per_group(arrived_group):
-        hidden = expand_rows(arrived_group[None], expert_gate_up)
-        return project_down(hidden, expert_down)[0].astype(jnp.bfloat16)
-
-    partial_out = lax.map(per_group, arrived)
-    returned = lax.all_to_all(
-        partial_out.reshape(groups * columns, local_experts * CAP, model_width),
+
+    all_rows = lax.all_gather(normed, ("req", "head"), axis=0, tiled=True)
+    local_experts = expert_gate_up.shape[0]
+    placing, slot_weight = slot_tables(
+        expert_ids, expert_weights, local_experts, token_rows, groups * columns
+    )
+    blocks = placing.shape[0]
+    slots = placing.shape[2]
+    block_rows = placing.shape[3]
+    slot_rows = jnp.einsum(
+        "bjst,btd->jbsd",
+        placing,
+        all_rows.reshape(blocks, block_rows, model_width),
+        preferred_element_type=jnp.float32,
+    ).astype(jnp.bfloat16)
+    slot_rows = slot_rows.reshape(local_experts, blocks * slots, model_width)
+    gate = jnp.einsum(
+        "jsd,jfd->jsf", slot_rows, expert_gate_up[:, 0], preferred_element_type=jnp.float32
+    )
+    up = jnp.einsum(
+        "jsd,jfd->jsf", slot_rows, expert_gate_up[:, 1], preferred_element_type=jnp.float32
+    )
+    hidden = (silu_mul(gate, up) * slot_weight[:, :, None]).astype(jnp.bfloat16)
+    down_out = jnp.einsum(
+        "jsf,jfd->jsd", hidden, expert_down, preferred_element_type=jnp.float32
+    ).astype(jnp.bfloat16)
+    partial_sum = jnp.einsum(
+        "bjst,jbsd->btd",
+        placing,
+        down_out.reshape(local_experts, blocks, slots, model_width),
+        preferred_element_type=jnp.float32,
+    ).astype(jnp.bfloat16)
+    routed = lax.psum_scatter(
+        partial_sum.reshape(groups * columns * token_rows, model_width),
         ("req", "head"),
-        split_axis=0,
-        concat_axis=0,
+        scatter_dimension=0,
         tiled=True,
-    )
-    summed = jnp.sum(returned.reshape(groups, slots_all, model_width).astype(jnp.float32), axis=0)
-    pair_rows = jnp.take(summed, slot_of, axis=0).reshape(token_rows, TOP, model_width)
-    routed = jnp.sum(pair_rows * expert_weights[:, :, None], axis=1)
+    ).astype(jnp.float32)
     return (mixed_rows + shared_out + routed).astype(jnp.bfloat16)
 
 

time: 491 us -> 336 us (0.68)
  waiting for transfers between devices: 298 us -> 152 us
  blocking collectives: 10.1 us -> 89.3 us
  local copies, waits for them, and re-layouts: 84 us -> 17.6 us
  other arithmetic: 15.4 us -> 4.1 us
  starting transfers between devices: 15.3 us -> 6.9 us
    all_to_all x2 -> x0, waiting for transfers between devices: 288 us -> none  [the longest x1 162 us: body(): lax.all_to_all(copies, ('req', 'head'), split_axis=0, concat_axis=0, tile...]
    reduce_scatter x0 -> x1, waiting for transfers between devices: none -> 142 us  [body(): lax.psum_scatter(partial_sum.reshape(groups * columns * token_rows, model...]
    all_gather x0 -> x2, blocking collectives: none -> 79.2 us  [the longest x1 40.9 us: slot_tables(): all_ids = lax.all_gather(expert_ids, ('req', 'head'), axis=0, tiled=True)]
    dot_general x1 -> x0, local copies, waits for them, and re-layouts: 15.1 us -> none  [body(): jnp.dot(normed, shared_gate_up.reshape(model_width, -1), preferred_elemen...]
    reduce_sum x3 -> x2, other arithmetic: 11.3 us -> 0.48 us  [the longest x1 0.35 us: slot_tables(): jnp.sum(jnp.where(placing, pair_weight[:, :, None, :], 0.0), axis=3)]
    reshape x2, local copies, waits for them, and re-layouts: 10.3 us -> 0.18 us  [the longest x1 0.1 us: slot_tables(): named = jnp.any(hit, axis=1).reshape(devices, token_rows, local_experts)]
    all_to_all x1 -> x0, local copies, waits for them, and re-layouts: 10.1 us -> none  [body(): lax.all_to_all(copies, ('req', 'head'), split_axis=0, concat_axis=0, tile...]
    dynamic_update_slice x4 -> x0, local copies, waits for them, and re-layouts: 8.94 us -> none  [body(): partial_out = lax.map(per_group, arrived)]
  transfers between devices with their start and end apart: 5 -> 5, of which waited for: 5 -> 4; matrix products, arithmetic and copies ran while one was open for 9% -> 4% of each run, Pallas kernels for 0% -> 0%
where the time goes in v1:
time: 336 us; the launch traced here: 335 us
  waiting for transfers between devices  152 us (45%)
  blocking collectives  89.3 us (27%)
  matrix products  51.5 us (15%)
  local copies, waits for them, and re-layouts  17.6 us (5%)
  between operations  13.4 us (4%)
  starting transfers between devices  6.9 us (2%)
  other arithmetic  4.1 us (1%)
    reduce_scatter x1, waiting for transfers between devices, body(): lax.psum_scatter(partial_sum.reshape(groups * columns * token_rows, model...  142 us
    all_gather x1, blocking collectives, slot_tables(): all_ids = lax.all_gather(expert_ids, ('req', 'head'), axis=0, tiled=True)  40.9 us
    all_gather x1, blocking collectives, slot_tables(): lax.all_gather(expert_weights, ('req', 'head'), axis=0, tiled=True)  38.3 us
    dot_general x1, matrix products, body(): jnp.einsum('jsf,jfd->jsd', hidden, expert_down, preferred_element_type=jn...  13.7 us
    all_to_all x1, blocking collectives, body(): lax.all_to_all(by_dest(keys_values), 'req', split_axis=0, concat_axis=0,...  10.1 us
    dot_general x1, matrix products, body(): jnp.einsum('bjst,jbsd->btd', placing, down_out.reshape(local_experts, blo...  8.69 us
    dot_general x1, matrix products, body(): jnp.einsum('bjst,btd->jbsd', placing, all_rows.reshape(blocks, block_rows...  8.46 us
  transfers between devices with their start and end apart: 5, of which 4 were waited for; matrix products, arithmetic and copies ran while one was open for 4% of the time, Pallas kernels for 0%

profile of v1, /device:TPU:0, one launch (start us, length us, event | category | flops | bytes accessed | tf_op | source)
XLA Modules:
  0.0 335.2 jit_solution(2674555757038372499)
XLA Ops:
  6.5 0.0 copy-start
  6.5 0.0 all-gather.5.cloned.1.call-start
  6.5 0.8 select_reduce_fusion.1
  7.4 1.5 gather_fusion
  8.9 0.1 broadcast_select_fusion.2
  8.9 10.1 %all_to_all.15 = bf16[4,16,1024]{2,1,0:T(8,128)(2,1)} all-to-all(bf16[4,16,1024]{2,1,0:T(8,128)(2,1)S(1)} %broadcast_select_fusion.2), channel_id=1, replica_groups=mesh['req'=4,'head'=8] {'req'}, dimensions={0} | all-to-all | bytes 262144 | tf_op jit(solution)/shard_map/all_to_all | solution.py:78
  19.0 0.0 all-gather.5.cloned.1.call-update
  19.1 0.0 copy-done
  19.1 0.6 gather_fusion.1
  19.7 1.5 gather_fusion.2
  21.2 0.9 broadcast_select_fusion.1
  22.1 3.4 %all-to-all-start = ((bf16[4,16,2048]{2,1,0:T(8,128)(2,1)}), bf16[4,16,2048]{2,1,0:T(8,128)(2,1)S(1)}, u32[]{:S(2)}, u32[]{:S(2)}) async-start(bf16[4,16,2048]{2,1,0:T(8,128)(2,1)} %get-tuple-element.40), calls=%async_computation | async-start | bytes 524288 | tf_op jit(solution)/shard_map/all_to_all | solution.py:76
  25.5 0.0 copy-done.8
  25.5 0.1 dynamic_slice.7
  25.6 5.2 %all-to-all-done = bf16[4,16,2048]{2,1,0:T(8,128)(2,1)S(1)} async-done(((bf16[4,16,2048]{2,1,0:T(8,128)(2,1)}), bf16[4,16,2048]{2,1,0:T(8,128)(2,1)S(1)}, u32[]{:S(2)}, u32[]{:S(2)}) %all-to-all-start) | async-done | bytes 262176 | tf_op jit(solution)/shard_map/all_to_all | solution.py:76
  30.8 3.4 %all-to-all-start.2 = ((bf16[4,16,2048]{2,1,0:T(8,128)(2,1)}), bf16[4,16,2048]{2,1,0:T(8,128)(2,1)S(1)}, u32[]{:S(2)}, u32[]{:S(2)}) async-start(bf16[4,16,2048]{2,1,0:T(8,128)(2,1)} %get-tuple-element.42), calls=%async_computation.2 | async-start | bytes 524288 | tf_op jit(solution)/shard_map/all_to_all | solution.py:77
  34.3 0.0 all-gather.7.cloned.1.call-start
  34.3 0.1 fusion.45
  34.4 1.2 reshape.143
  35.6 4.0 %all-to-all-done.2 = bf16[4,16,2048]{2,1,0:T(8,128)(2,1)S(1)} async-done(((bf16[4,16,2048]{2,1,0:T(8,128)(2,1)}), bf16[4,16,2048]{2,1,0:T(8,128)(2,1)S(1)}, u32[]{:S(2)}, u32[]{:S(2)}) %all-to-all-start.2) | async-done | bytes 262176 | tf_op jit(solution)/shard_map/all_to_all | solution.py:77
  39.6 0.9 reshape_reshape.3
  40.5 0.6 all-gather.5.cloned.1.call-done
  41.0 1.3 fusion.61
  42.3 0.2 copy.87
  42.5 1.5 fusion.14
  44.0 0.0 copy-start.4
  44.0 0.7 fusion.19
  44.8 1.0 copy.90
  45.8 0.0 copy-done.4
  45.8 2.0 fusion.36
  47.8 0.0 copy-start.6
  47.8 0.0 copy-start.7
  47.8 0.3 copy.92
  48.1 0.2 reshape.134
  48.4 0.0 copy-done.5
  48.4 0.8 multiply_convert_fusion.1
  49.2 0.0 all-gather.7.cloned.1.call-update
  49.2 0.0 reduce-scatter.2.cloned.1.call-start
  49.3 0.0 copy-done.6
  49.3 40.9 %all-gather = s32[32,64,6]{1,2,0:T(8,128)S(1)} all-gather(s32[1,64,6]{1,2,0:T(8,128)S(1)} %bitcast.138), channel_id=1, replica_groups=mesh['req'=4,'head'=8] {'req','head'}, dimensions={0}, use_global_device_ids=true | all-gather | bytes 50688 | tf_op jit(solution)/shard_map/all_gather | solution.py:22
  90.2 0.1 reshape.171
  90.3 0.1 compare_reduce_fusion
  90.4 0.1 reshape.135
  90.5 0.2 fusion.27
  90.8 0.1 reshape.136
  90.9 0.0 copy-done.7
  90.9 38.3 %all-gather.1 = f32[32,64,6]{1,2,0:T(8,128)S(1)} all-gather(f32[1,64,6]{1,2,0:T(8,128)S(1)} %bitcast.139), channel_id=1, replica_groups=mesh['req'=4,'head'=8] {'req','head'}, dimensions={0}, use_global_device_ids=true | all-gather | bytes 50688 | tf_op jit(solution)/shard_map/all_gather | solution.py:23
  129.2 0.1 reshape.173
  129.3 0.1 fusion.42
  129.4 0.4 select_reduce_fusion
  129.8 0.1 mul.112
  129.9 0.0 all-gather.7.cloned.1.call-done
  129.9 8.5 %convert_bitcast_fusion = bf16[4,8,56,2048]{3,2,0,1:T(8,128)(2,1)} fusion(bf16[8,256,2048,1]{2,1,3,0:T(8,128)(2,1)} %bitcast.140, s32[8,4,256]{2,1,0:T(4,128)S(1)} %copy.96), kind=kOutput, calls=%fused_computation.8 | convolution fusion | flops 1883176960 | bytes 15761408 | tf_op jit(solution)/shard_map/bjst,btd->jbsd/dot_general | solution.py:156
  138.4 4.5 %copy.97 = bf16[4,8,56,2048]{3,2,1,0:T(8,128)(2,1)S(1)} copy(bf16[4,8,56,2048]{3,2,0,1:T(8,128)(2,1)} %convert_bitcast_fusion) | data formatting | bytes 14680064 | tf_op jit(solution)/shard_map/convert_element_type | solution.py:161
  142.9 0.0 copy-start.2
  142.9 2.9 copy-done.2
  145.8 6.0 %fusion.6 = f32[4,448,352]{2,1,0:T(8,128)S(1)} fusion(bf16[4,448,2048]{2,1,0:T(8,128)(2,1)S(1)} %bitcast.127, bf16[4,2,352,2048]{3,2,1,0:T(8,128)(2,1)} %param.24), kind=kOutput, calls=%fused_computation.11 | convolution fusion | flops 2583691264 | bytes 15630336 | tf_op jit(solution)/shard_map/jsd,jfd->jsf/dot_general | solution.py:163
  151.8 13.7 %convolution_convert_fusion = bf16[4,448,2048]{2,1,0:T(8,128)(2,1)} fusion(bf16[4,352,2048]{2,1,0:T(8,128)(2,1)} %param.25, f32[4,448,352]{2,1,0:T(8,128)S(1)} %fusion.6, bf16[4,448,2048]{2,1,0:T(8,128)(2,1)} %bitcast.128, bf16[4,2,352,2048]{3,2,1,0:T(8,128)(2,1)} %param.24, f32[4,448]{1,0:T(4,128)S(1)} %mul.112), kind=kOutput, calls=%fused_computation.15 | convolution fusion | flops 5174837248 | bytes 28744704 | tf_op jit(solution)/shard_map/jsf,jfd->jsd/dot_general | solution.py:170
  165.4 8.7 %bitcast_convert_fusion = bf16[8,256,2048]{2,1,0:T(8,128)(2,1)} fusion(bf16[4,8,56,2048]{3,2,1,0:T(8,128)(2,1)} %bitcast.142, s32[8,4,256]{2,1,0:T(4,128)S(1)} %copy.96), kind=kOutput, calls=%fused_computation.3 | convolution fusion | flops 1883701248 | bytes 15761408 | tf_op jit(solution)/shard_map/bjst,jbsd->btd/dot_general | solution.py:173
  174.1 0.0 reduce-scatter.2.cloned.1.call-update
  174.2 0.9 copy-done.3
  175.1 6.6 %fusion = f32[64,2,1408]{2,0,1:T(8,128)S(1)} fusion(bf16[2048,2,1408]{2,1,0:T(2,128)(2,1)} %param.22, bf16[64,2048]{1,0:T(8,128)(2,1)S(1)} %copy-done.3), kind=kOutput, calls=%fused_computation.4 | convolution fusion | flops 738197504 | bytes 12517376 | tf_op jit(solution)/shard_map/td,dcf->tcf/dot_general | solution.py:142
  181.7 142.5 %reduce-scatter.2.cloned.1.call-done = bf16[64,2048]{1,0:T(8,128)(2,1)} async-done(((bf16[2048,2048]{1,0:T(8,128)(2,1)}), bf16[64,2048]{1,0:T(8,128)(2,1)}) %reduce-scatter.2.cloned.1.call-update) | async-done | bytes 262160 | tf_op jit(solution)/shard_map/reduce_scatter | solution.py:179
  324.2 4.5 %fusion.13 = bf16[64,2048]{1,0:T(8,128)(2,1)} fusion(f32[64,2048]{1,0:T(8,128)S(1)} %get-tuple-element.25, bf16[1408,2048]{1,0:T(8,128)(2,1)} %param.23, bf16[64,2048]{1,0:T(8,128)(2,1)} %reduce-scatter.2.cloned.1.call-done, f32[64,2,1408]{2,0,1:T(8,128)S(1)} %fusion), kind=kOutput, calls=%fused_computation.19 | convolution fusion | flops 370073600 | bytes 7536640 | tf_op jit(solution)/shard_map/dot_general | solution.py:146
  (23 shorter events, 0.2 us)
Async XLA Ops:
  6.5 12.6 %copy-start = (bf16[64,2048]{1,0:T(8,128)(2,1)S(1)}, bf16[64,2048]{1,0:T(8,128)(2,1)}, u32[]{:S(2)}) copy-start(bf16[64,2048]{1,0:T(8,128)(2,1)} %param.14) | copy-start | bytes 786436
  6.5 19.0 %copy-start.8 = (s32[512]{0:T(512)S(1)}, s32[512]{0:T(512)}, u32[]{:S(2)}) copy-start(s32[512]{0:T(512)} %param.17) | copy-start | bytes 6148
  6.5 34.5 %all-gather.5.cloned.1.call-start = ((), (), s32[]{:S(2)}) async-start(), calls=%async_computation.4 | async-start | bytes 1179648 | tf_op jit(solution)/shard_map/all_gather | solution.py:95
  22.1 8.8 %all-to-all-start = ((bf16[4,16,2048]{2,1,0:T(8,128)(2,1)}), bf16[4,16,2048]{2,1,0:T(8,128)(2,1)S(1)}, u32[]{:S(2)}, u32[]{:S(2)}) async-start(bf16[4,16,2048]{2,1,0:T(8,128)(2,1)} %get-tuple-element.40), calls=%async_computation | async-start | bytes 524288 | tf_op jit(solution)/shard_map/all_to_all | solution.py:76
  30.8 8.8 %all-to-all-start.2 = ((bf16[4,16,2048]{2,1,0:T(8,128)(2,1)}), bf16[4,16,2048]{2,1,0:T(8,128)(2,1)S(1)}, u32[]{:S(2)}, u32[]{:S(2)}) async-start(bf16[4,16,2048]{2,1,0:T(8,128)(2,1)} %get-tuple-element.42), calls=%async_computation.2 | async-start | bytes 524288 | tf_op jit(solution)/shard_map/all_to_all | solution.py:77
  34.3 95.7 %all-gather.7.cloned.1.call-start = ((), (), s32[]{:S(2)}) async-start(), calls=%async_computation.5 | async-start | bytes 8650752 | tf_op jit(solution)/shard_map/all_gather | solution.py:148
  44.0 1.8 copy-start.4
  45.8 2.6 copy-start.5
  47.8 1.5 copy-start.6
  47.8 43.1 %copy-start.7 = (f32[64,6]{0,1:T(8,128)S(1)}, f32[64,6]{0,1:T(8,128)}, u32[]{:S(2)}) copy-start(f32[64,6]{0,1:T(8,128)} %param.20) | copy-start | bytes 4612
  49.2 274.9 %reduce-scatter.2.cloned.1.call-start = ((), (), s32[]{:S(2)}) async-start(), calls=%async_computation.6 | async-start | bytes 8650752 | tf_op jit(solution)/shard_map/reduce_scatter | solution.py:179
  142.9 3.0 copy-start.2
  174.1 0.9 copy-start.3
  324.2 4.5 %copy-start.1 = (bf16[64,2048]{1,0:T(8,128)(2,1)S(1)}, bf16[64,2048]{1,0:T(8,128)(2,1)}, u32[]{:S(2)}) copy-start(bf16[64,2048]{1,0:T(8,128)(2,1)} %param.14) | copy-start | bytes 786436
Sparse Core Ops, SparseCore 0:
  19.2 21.8 all-gather.4
  49.3 77.2 all-gather.6
  174.3 149.8 reduce-scatter.1

commit v2 on v1

--- a/solution.py
+++ b/solution.py
@@ -1,6 +1,10 @@
+import functools
+
 import jax
 import jax.numpy as jnp
 from jax import lax
+from jax.experimental import pallas as pl
+from jax.experimental.pallas import tpu as pltpu
 from jax.sharding import PartitionSpec as P
 
 QUERY_HEADS = 16
@@ -18,9 +22,232 @@
     return gate_value / (1.0 + jnp.exp(-gate_value)) * upward
 
 
-def slot_tables(expert_ids, expert_weights, local_experts, token_rows, devices):
-    all_ids = lax.all_gather(expert_ids, ("req", "head"), axis=0, tiled=True)
-    all_weights = lax.all_gather(expert_weights, ("req", "head"), axis=0, tiled=True)
+def places():
+    r, h = lax.axis_index("req"), lax.axis_index("head")
+    return lax.div(r, 2), lax.rem(r, 2), lax.div(h, 2), lax.rem(h, 2)
+
+
+def partners(zs):
+    y, x, z, c = places()
+    r, h = y * 2 + x, z * 2 + c
+    x_dev = (y * 2 + 1 - x, h)
+    y_dev = ((1 - y) * 2 + x, h)
+    sibling = (r, z * 2 + 1 - c)
+    z_devs = [(r, lax.rem(z + k, zs) * 2 + c) for k in range(zs)]
+    return x_dev, y_dev, sibling, z_devs
+
+
+def greet(devices):
+    barrier = pltpu.get_barrier_semaphore()
+    for device in devices:
+        pl.semaphore_signal(
+            barrier, inc=1, device_id=device, device_id_type=pl.DeviceIdType.MESH
+        )
+    pl.semaphore_wait(barrier, len(devices))
+
+
+def send(src, dst, send_sem, recv_sem, device):
+    return pltpu.make_async_remote_copy(
+        src_ref=src,
+        dst_ref=dst,
+        send_sem=send_sem,
+        recv_sem=recv_sem,
+        device_id=device,
+        device_id_type=pl.DeviceIdType.MESH,
+    )
+
+
+def gather_kernel(zs, n_ref, m_ref, g_ref, w_ref, own, zss, zsr, xs, xr, ys, yr, das, dar, dbs, dbr, ss, sr):
+    y, x, z, c = places()
+    x_dev, y_dev, sibling, z_devs = partners(zs)
+    greet([x_dev, y_dev, sibling] + z_devs[1:])
+    pairs = ((n_ref, g_ref), (m_ref, w_ref))
+    started = []
+
+    def go(copy):
+        copy.start()
+        started.append(copy)
+        return copy
+
+    local = []
+    for a, (src, full) in enumerate(pairs):
+        for k in range(1, zs):
+            go(send(src, full.at[y, x, z, c], zss.at[a, k], zsr.at[a, k], z_devs[k]))
+        copy = pltpu.make_async_copy(src, full.at[y, x, z, c], own.at[a])
+        copy.start()
+        local.append(copy)
+
+    def arrived(ref, sem):
+        send(ref, ref, sem, sem, sibling).wait_recv()
+
+    for step in range(zs + 2):
+        if step < zs:
+            zk = lax.rem(z - step + zs, zs)
+            for a, (src, full) in enumerate(pairs):
+                block = full.at[y, x, zk, c]
+                if step > 0:
+                    arrived(block, zsr.at[a, step])
+                    src = block
+                go(send(src, block, xs.at[a, step], xr.at[a, step], x_dev))
+                go(send(src, block, ys.at[a, step], yr.at[a, step], y_dev))
+        if 1 <= step <= zs:
+            k = step - 1
+            zk = lax.rem(z - k + zs, zs)
+            for a, (src, full) in enumerate(pairs):
+                half = src.shape[0] // 2
+                arrived(full.at[y, 1 - x, zk, c], xr.at[a, k])
+                part = full.at[y, 1 - x, zk, c, pl.ds(0, half)]
+                go(send(part, part, das.at[a, k], dar.at[a, k], y_dev))
+                arrived(full.at[1 - y, x, zk, c], yr.at[a, k])
+                part = full.at[1 - y, x, zk, c, pl.ds(half, half)]
+                go(send(part, part, dbs.at[a, k], dbr.at[a, k], x_dev))
+        if step >= 2:
+            k = step - 2
+            zk = lax.rem(z - k + zs, zs)
+            for a, (src, full) in enumerate(pairs):
+                half = src.shape[0] // 2
+                if k == 0:
+                    local[a].wait()
+                arrived(full.at[1 - y, 1 - x, zk, c, pl.ds(0, half)], dar.at[a, k])
+                arrived(full.at[1 - y, 1 - x, zk, c, pl.ds(half, half)], dbr.at[a, k])
+                part = full.at[:, :, zk, c]
+                go(send(part, part, ss.at[a, k], sr.at[a, k], sibling))
+    for k in range(zs):
+        zk = lax.rem(z - k + zs, zs)
+        for a, (src, full) in enumerate(pairs):
+            arrived(full.at[:, :, zk, 1 - c], sr.at[a, k])
+    for copy in started:
+        copy.wait_send()
+
+
+def gather_all(rows, meta, zs):
+    shape = (2, 2, zs, 2)
+    sems = pltpu.SemaphoreType.DMA((2, zs))
+    return pl.pallas_call(
+        functools.partial(gather_kernel, zs),
+        out_shape=(
+            jax.ShapeDtypeStruct(shape + rows.shape, rows.dtype),
+            jax.ShapeDtypeStruct(shape + meta.shape, meta.dtype),
+        ),
+        in_specs=[pl.BlockSpec(memory_space=pltpu.VMEM)] * 2,
+        out_specs=(pl.BlockSpec(memory_space=pl.ANY), pl.BlockSpec(memory_space=pl.ANY)),
+        scratch_shapes=[pltpu.SemaphoreType.DMA((2,))] + [sems] * 12,
+        compiler_params=pltpu.CompilerParams(
+            collective_id=0, has_side_effects=True, vmem_limit_bytes=32 << 20
+        ),
+    )(rows, meta)
+
+
+def scatter_kernel(zs, p_ref, o_ref, r1, r2a, r2b, r3a, r3b, s3, r4, sems):
+    y, x, z, c = places()
+    x_dev, y_dev, sibling, z_devs = partners(zs)
+    greet([x_dev, y_dev, sibling] + z_devs[1:])
+    rows = o_ref.shape[0]
+    half = rows // 2
+    strip = 16
+    started = []
+
+    def go(src, dst, kind, k, device):
+        copy = send(src, dst, sems.at[0, kind, k], sems.at[1, kind, k], device)
+        copy.start()
+        started.append(copy)
+        return copy
+
+    def arrived(ref, kind, k):
+        send(ref, ref, sems.at[0, kind, k], sems.at[1, kind, k], sibling).wait_recv()
+
+    for k in range(zs):
+        zk = lax.rem(z + 1 + k, zs)
+        go(p_ref.at[:, :, zk, 1 - c], r1.at[k], 0, k, sibling)
+
+    for step in range(zs + 2):
+        if step < zs:
+            k = step
+            zk = lax.rem(z + 1 + k, zs)
+            arrived(r1.at[k], 0, k)
+            strips = rows // strip
+
+            @pl.loop(0, 4 * strips)
+            def _(i):
+                group = lax.div(i, strips)
+                b, a = lax.div(group, 2), lax.rem(group, 2)
+                span = pl.ds(lax.rem(i, strips) * strip, strip)
+                r1[k, b, a, span, :] = r1[k, b, a, span, :] + p_ref[b, a, zk, c, span, :]
+
+            go(r1.at[k, 1 - y, :, pl.ds(0, half)], r2a.at[k], 1, k, y_dev)
+            go(r1.at[k, :, 1 - x, pl.ds(half, half)], r2b.at[k], 2, k, x_dev)
+        if 1 <= step <= zs:
+            k = step - 1
+            strips = half // strip
+            arrived(r2a.at[k], 1, k)
+            arrived(r2b.at[k], 2, k)
+
+            @pl.loop(0, 2 * strips)
+            def _(i):
+                a = lax.div(i, strips)
+                start = lax.rem(i, strips) * strip
+                span, low = pl.ds(start, strip), pl.ds(half + start, strip)
+                r2a[k, a, span, :] = r2a[k, a, span, :] + r1[k, y, a, span, :]
+                r2b[k, a, span, :] = r2b[k, a, span, :] + r1[k, a, x, low, :]
+
+            go(r2a.at[k, 1 - x], r3a.at[k], 3, k, x_dev)
+            go(r2b.at[k, 1 - y], r3b.at[k], 4, k, y_dev)
+        if step >= 2:
+            k = step - 2
+            strips = half // strip
+            arrived(r3a.at[k], 3, k)
+            arrived(r3b.at[k], 4, k)
+
+            @pl.loop(0, strips)
+            def _(i):
+                start = i * strip
+                span, low = pl.ds(start, strip), pl.ds(half + start, strip)
+                s3[k, span, :] = r3a[k, span, :] + r2a[k, x, span, :]
+                s3[k, low, :] = r3b[k, span, :] + r2b[k, y, span, :]
+
+            if k < zs - 1:
+                go(s3.at[k], r4.at[k], 5, k, z_devs[k + 1])
+    for k in range(zs - 1):
+        arrived(r4.at[k], 5, k)
+
+    @pl.loop(0, rows // strip)
+    def _(i):
+        span = pl.ds(i * strip, strip)
+        total = s3[zs - 1, span, :].astype(jnp.float32)
+        for k in range(zs - 1):
+            total = total + r4[k, span, :].astype(jnp.float32)
+        o_ref[span, :] = total
+
+    for copy in started:
+        copy.wait_send()
+
+
+def scatter_sum(partial_sum, zs, rows):
+    width = partial_sum.shape[-1]
+    half = rows // 2
+    bf16 = partial_sum.dtype
+    return pl.pallas_call(
+        functools.partial(scatter_kernel, zs),
+        out_shape=jax.ShapeDtypeStruct((rows, width), jnp.float32),
+        in_specs=[pl.BlockSpec(memory_space=pltpu.VMEM)],
+        out_specs=pl.BlockSpec(memory_space=pltpu.VMEM),
+        scratch_shapes=[
+            pltpu.VMEM((zs, 2, 2, rows, width), bf16),
+            pltpu.VMEM((zs, 2, half, width), bf16),
+            pltpu.VMEM((zs, 2, half, width), bf16),
+            pltpu.VMEM((zs, half, width), bf16),
+            pltpu.VMEM((zs, half, width), bf16),
+            pltpu.VMEM((zs, rows, width), bf16),
+            pltpu.VMEM((zs - 1, rows, width), bf16),
+            pltpu.SemaphoreType.DMA((2, 6, zs)),
+        ],
+        compiler_params=pltpu.CompilerParams(
+            collective_id=1, has_side_effects=True, vmem_limit_bytes=48 << 20
+        ),
+    )(partial_sum.reshape(2, 2, zs, 2, rows, width))
+
+
+def slot_tables(all_ids, all_weights, local_experts, token_rows, devices):
     first = lax.axis_index("head") * local_experts
     mine = first + jnp.arange(local_experts, dtype=jnp.int32)
     hit = all_ids[:, :, None] == mine[None, None, :]
@@ -145,10 +372,23 @@
     shared_hidden = silu_mul(shared_both[:, 0], shared_both[:, 1]).astype(jnp.bfloat16)
     shared_out = jnp.dot(shared_hidden, shared_down, preferred_element_type=jnp.float32)
 
-    all_rows = lax.all_gather(normed, ("req", "head"), axis=0, tiled=True)
+    devices = groups * columns
+    by_kernel = groups == 4 and columns * groups * normed.size * 2 <= 16 << 20
+    if by_kernel:
+        meta = jnp.concatenate([expert_ids.astype(jnp.float32), expert_weights], axis=1).T
+        meta = jnp.pad(meta, ((0, 16 - 2 * TOP), (0, -token_rows % 128)))
+        all_rows, all_meta = gather_all(normed, meta, columns // 2)
+        all_meta = all_meta.reshape(devices, meta.shape[0], meta.shape[1])[:, :, :token_rows]
+        all_meta = jnp.transpose(all_meta, (0, 2, 1)).reshape(devices * token_rows, -1)
+        all_ids = all_meta[:, :TOP].astype(jnp.int32)
+        all_weights = all_meta[:, TOP : 2 * TOP]
+    else:
+        all_rows = lax.all_gather(normed, ("req", "head"), axis=0, tiled=True)
+        all_ids = lax.all_gather(expert_ids, ("req", "head"), axis=0, tiled=True)
+        all_weights = lax.all_gather(expert_weights, ("req", "head"), axis=0, tiled=True)
     local_experts = expert_gate_up.shape[0]
     placing, slot_weight = slot_tables(
-        expert_ids, expert_weights, local_experts, token_rows, groups * columns
+        all_ids, all_weights, local_experts, token_rows, devices
     )
     blocks = placing.shape[0]
     slots = placing.shape[2]
@@ -176,12 +416,15 @@
         down_out.reshape(local_experts, blocks, slots, model_width),
         preferred_element_type=jnp.float32,
     ).astype(jnp.bfloat16)
-    routed = lax.psum_scatter(
-        partial_sum.reshape(groups * columns * token_rows, model_width),
-        ("req", "head"),
-        scatter_dimension=0,
-        tiled=True,
-    ).astype(jnp.float32)
+    if by_kernel:
+        routed = scatter_sum(partial_sum, columns // 2, token_rows)
+    else:
+        routed = lax.psum_scatter(
+            partial_sum.reshape(devices * token_rows, model_width),
+            ("req", "head"),
+            scatter_dimension=0,
+            tiled=True,
+        ).astype(jnp.float32)
     return (mixed_rows + shared_out + routed).astype(jnp.bfloat16)
 
 

time: 336 us -> 223 us (0.66)
  waiting for transfers between devices: 152 us -> 10.5 us
  Pallas kernels: 0 us -> 106 us
  blocking collectives: 89.3 us -> 10.1 us
    reduce_scatter x1 -> x0, waiting for transfers between devices: 142 us -> none  [body(): lax.psum_scatter(partial_sum.reshape(groups * columns * token_rows, model...]
    pallas_call x0 -> x2, Pallas kernels: none -> 106 us  [the longest x1 56 us: scatter_sum(): pl.pallas_call(functools.partial(scatter_kernel, zs), out_shape=jax.Shape...]
    all_gather x2 -> x0, blocking collectives: 79.2 us -> none  [the longest x1 40.9 us: slot_tables(): all_ids = lax.all_gather(expert_ids, ('req', 'head'), axis=0, tiled=True)]
  transfers between devices with their start and end apart: 5 -> 3, of which waited for: 4 -> 3; matrix products, arithmetic and copies ran while one was open for 4% -> 2% of each run, Pallas kernels for 0% -> 0%
where the time goes in v2:
time: 223 us
  Pallas kernels  106 us (48%)
  matrix products  51.7 us (23%)
  local copies, waits for them, and re-layouts  20 us (9%)
  between operations  13.8 us (6%)
  waiting for transfers between devices  10.5 us (5%)
  blocking collectives  10.1 us (5%)
  starting transfers between devices  6.84 us (3%)
  other arithmetic  3.44 us (2%)
    pallas_call x1, Pallas kernels, scatter_sum(): pl.pallas_call(functools.partial(scatter_kernel, zs), out_shape=jax.Shape...  56 us
    pallas_call x1, Pallas kernels, gather_all(): pl.pallas_call(functools.partial(gather_kernel, zs), out_shape=(jax.Shape...  50.4 us
    dot_general x1, matrix products, body(): jnp.einsum('jsf,jfd->jsd', hidden, expert_down, preferred_element_type=jn...  14 us
    all_to_all x1, blocking collectives, body(): lax.all_to_all(by_dest(keys_values), 'req', split_axis=0, concat_axis=0,...  10.1 us
    dot_general x1, matrix products, body(): jnp.einsum('bjst,jbsd->btd', placing, down_out.reshape(local_experts, blo...  8.77 us
    dot_general x1, matrix products, body(): jnp.einsum('bjst,btd->jbsd', placing, all_rows.reshape(blocks, block_rows...  8.45 us
    dot_general x1, matrix products, body(): jnp.einsum('jsd,jfd->jsf', slot_rows, expert_gate_up[:, 0], preferred_ele...  8.08 us
    dot_general x1, matrix products, body(): jnp.einsum('td,dcf->tcf', normed, shared_gate_up, preferred_element_type=...  6.5 us
  transfers between devices with their start and end apart: 3, of which 3 were waited for; matrix products, arithmetic and copies ran while one was open for 2% of the time, Pallas kernels for 0%

profile of v2, /device:TPU:0, one launch (start us, length us, event | category | flops | bytes accessed | tf_op | source)
XLA Modules:
  0.0 222.8 jit_solution(12626892351384320604)
XLA Ops:
  6.5 0.0 copy-start
  6.5 0.0 copy-start.7
  6.5 0.0 copy-start.6
  6.5 0.0 all-gather.2.cloned.1.call-start
  6.6 0.8 select_reduce_fusion.1
  7.4 1.5 gather_fusion
  8.9 0.1 broadcast_select_fusion.2
  9.0 10.1 %all_to_all.15 = bf16[4,16,1024]{2,1,0:T(8,128)(2,1)} all-to-all(bf16[4,16,1024]{2,1,0:T(8,128)(2,1)S(1)} %broadcast_select_fusion.2), channel_id=1, replica_groups=mesh['req'=4,'head'=8] {'req'}, dimensions={0} | all-to-all | bytes 262144 | tf_op jit(solution)/shard_map/all_to_all | solution.py:305
  19.1 0.0 all-gather.2.cloned.1.call-update
  19.1 0.0 copy-done
  19.1 0.6 gather_fusion.1
  19.7 1.5 gather_fusion.2
  21.2 0.9 broadcast_select_fusion.1
  22.1 3.4 %all-to-all-start.2 = ((bf16[4,16,2048]{2,1,0:T(8,128)(2,1)}), bf16[4,16,2048]{2,1,0:T(8,128)(2,1)S(1)}, u32[]{:S(2)}, u32[]{:S(2)}) async-start(bf16[4,16,2048]{2,1,0:T(8,128)(2,1)} %get-tuple-element.49), calls=%async_computation.2 | async-start | bytes 524288 | tf_op jit(solution)/shard_map/all_to_all | solution.py:304
  25.5 0.0 copy-done.5
  25.6 0.0 copy-done.7
  25.6 0.1 dynamic_slice.7
  25.7 0.0 copy-done.6
  25.7 5.1 %all-to-all-done.2 = bf16[4,16,2048]{2,1,0:T(8,128)(2,1)S(1)} async-done(((bf16[4,16,2048]{2,1,0:T(8,128)(2,1)}), bf16[4,16,2048]{2,1,0:T(8,128)(2,1)S(1)}, u32[]{:S(2)}, u32[]{:S(2)}) %all-to-all-start.2) | async-done | bytes 262176 | tf_op jit(solution)/shard_map/all_to_all | solution.py:304
  30.9 3.4 %all-to-all-start = ((bf16[4,16,2048]{2,1,0:T(8,128)(2,1)}), bf16[4,16,2048]{2,1,0:T(8,128)(2,1)S(1)}, u32[]{:S(2)}, u32[]{:S(2)}) async-start(bf16[4,16,2048]{2,1,0:T(8,128)(2,1)} %get-tuple-element.48), calls=%async_computation | async-start | bytes 524288 | tf_op jit(solution)/shard_map/all_to_all | solution.py:303
  34.3 0.1 fusion.45
  34.4 0.2 reshape_reshape.3
  34.6 5.1 %all-to-all-done = bf16[4,16,2048]{2,1,0:T(8,128)(2,1)S(1)} async-done(((bf16[4,16,2048]{2,1,0:T(8,128)(2,1)}), bf16[4,16,2048]{2,1,0:T(8,128)(2,1)S(1)}, u32[]{:S(2)}, u32[]{:S(2)}) %all-to-all-start) | async-done | bytes 262176 | tf_op jit(solution)/shard_map/all_to_all | solution.py:303
  39.6 1.2 reshape.151
  40.8 0.3 all-gather.2.cloned.1.call-done
  41.1 1.3 fusion.61
  42.3 1.0 copy.84
  43.4 1.6 fusion.14
  44.9 0.7 fusion.19
  45.7 1.0 copy.87
  46.7 0.0 copy-start.4
  46.7 2.2 fusion.36
  48.9 0.3 copy.89
  49.2 0.2 reshape.140
  49.5 0.0 copy-done.4
  49.5 0.1 multiply_convert_fusion.1
  49.6 50.4 %shard_map.118 = (bf16[2,2,4,2,64,2048]{5,4,3,2,1,0:T(8,128)(2,1)S(1)}, f32[2,2,4,2,16,128]{5,4,3,2,1,0:T(8,128)S(1)}) custom-call(bf16[64,2048]{1,0:T(8,128)(2,1)S(1)} %get-tuple-element.28.n_ref, f32[16,128]{1,0:T(8,128)S(1)} %pad.4.m_ref), custom_call_target="tpu_custom_call" | custom-call | tf_op jit(solution)/shard_map/pallas_call | solution.py:126
  100.0 0.0 copy-start.2
  100.1 3.2 %copy-done.2 = bf16[2,2,4,2,64,2048]{5,4,3,2,1,0:T(8,128)(2,1)} copy-done((bf16[2,2,4,2,64,2048]{5,4,3,2,1,0:T(8,128)(2,1)}, bf16[2,2,4,2,64,2048]{5,4,3,2,1,0:T(8,128)(2,1)S(1)}, u32[]{:S(2)}) %copy-start.2) | copy-done | bytes 8388632
  103.3 0.1 copy.129
  103.4 0.1 reshape.142
  103.5 0.1 compare_reduce_fusion
  103.6 0.1 fusion.42
  103.8 0.1 reshape.143
  103.9 0.2 fusion.27
  104.1 0.1 reshape.144
  104.2 0.4 select_reduce_fusion
  104.6 0.1 mul.112
  104.7 8.4 %convert_bitcast_fusion = bf16[4,8,56,2048]{3,2,0,1:T(8,128)(2,1)} fusion(bf16[8,256,2048,1]{2,1,3,0:T(8,128)(2,1)} %bitcast.130, s32[8,4,256]{2,1,0:T(4,128)S(1)} %copy.93), kind=kOutput, calls=%fused_computation.8 | convolution fusion | flops 1883176960 | bytes 15761408 | tf_op jit(solution)/shard_map/bjst,btd->jbsd/dot_general | solution.py:396
  113.1 4.5 %copy.94 = bf16[4,8,56,2048]{3,2,1,0:T(8,128)(2,1)S(1)} copy(bf16[4,8,56,2048]{3,2,0,1:T(8,128)(2,1)} %convert_bitcast_fusion) | data formatting | bytes 14680064 | tf_op jit(solution)/shard_map/convert_element_type | solution.py:401
  117.6 0.0 copy-start.3
  117.6 3.0 %copy-done.3 = bf16[4,8,56,2048]{3,2,1,0:T(8,128)(2,1)} copy-done((bf16[4,8,56,2048]{3,2,1,0:T(8,128)(2,1)}, bf16[4,8,56,2048]{3,2,1,0:T(8,128)(2,1)S(1)}, u32[]{:S(2)}) %copy-start.3) | copy-done | bytes 7340056
  120.6 8.1 %fusion.6 = f32[4,448,352]{2,1,0:T(8,128)} fusion(bf16[4,448,2048]{2,1,0:T(8,128)(2,1)S(1)} %bitcast.132, bf16[4,2,352,2048]{3,2,1,0:T(8,128)(2,1)} %param.24), kind=kOutput, calls=%fused_computation.11 | convolution fusion | flops 2583691264 | bytes 15630336 | tf_op jit(solution)/shard_map/jsd,jfd->jsf/dot_general | solution.py:403
  128.7 14.0 %convolution_convert_fusion = bf16[4,448,2048]{2,1,0:T(8,128)(2,1)} fusion(bf16[4,352,2048]{2,1,0:T(8,128)(2,1)} %param.25, f32[4,448,352]{2,1,0:T(8,128)} %fusion.6, bf16[4,448,2048]{2,1,0:T(8,128)(2,1)} %bitcast.133, bf16[4,2,352,2048]{3,2,1,0:T(8,128)(2,1)} %param.24, f32[4,448]{1,0:T(4,128)S(1)} %mul.112), kind=kOutput, calls=%fused_computation.15 | convolution fusion | flops 5174837248 | bytes 28974080 | tf_op jit(solution)/shard_map/jsf,jfd->jsd/dot_general | solution.py:410
  142.7 8.8 %bitcast_convert_fusion = bf16[8,256,2048]{2,1,0:T(8,128)(2,1)} fusion(bf16[4,8,56,2048]{3,2,1,0:T(8,128)(2,1)} %bitcast.147, s32[8,4,256]{2,1,0:T(4,128)S(1)} %copy.93), kind=kOutput, calls=%fused_computation.3 | convolution fusion | flops 1883701248 | bytes 15761408 | tf_op jit(solution)/shard_map/bjst,jbsd->btd/dot_general | solution.py:413
  151.5 0.0 slice-start
  151.5 56.0 %shard_map.119 = f32[64,2048]{1,0:T(8,128)S(1)} custom-call(bf16[2,2,4,2,64,2048]{5,4,3,2,1,0:T(8,128)(2,1)} %bitcast.131), custom_call_target="tpu_custom_call" | custom-call | tf_op jit(solution)/shard_map/pallas_call | solution.py:229
  207.5 0.0 slice-start.1
  207.5 6.5 %fusion = f32[64,2,1408]{2,0,1:T(8,128)S(1)} fusion(bf16[2048,2,1408]{2,1,0:T(2,128)(2,1)} %param.22, bf16[64,2048]{1,0:T(8,128)(2,1)S(1)} %get-tuple-element.28.n_ref), kind=kOutput, calls=%fused_computation.4 | convolution fusion | flops 738197504 | bytes 12517376 | tf_op jit(solution)/shard_map/td,dcf->tcf/dot_general | solution.py:369
  214.1 0.0 copy-start.1
  214.1 0.0 slice-done
  214.1 0.0 slice-done.1
  214.1 1.8 fusion.13
  215.9 0.0 copy-done.1
  (22 shorter events, 0.2 us)
Async XLA Ops:
  6.5 12.6 %copy-start = (bf16[64,2048]{1,0:T(8,128)(2,1)S(1)}, bf16[64,2048]{1,0:T(8,128)(2,1)}, u32[]{:S(2)}) copy-start(bf16[64,2048]{1,0:T(8,128)(2,1)} %param.14) | copy-start | bytes 786436
  6.5 19.0 %copy-start.5 = (s32[64,6]{0,1:T(8,128)S(1)}, s32[64,6]{0,1:T(8,128)}, u32[]{:S(2)}) copy-start(s32[64,6]{0,1:T(8,128)} %param.19) | copy-start | bytes 4612
  6.5 19.0 %copy-start.7 = (s32[512]{0:T(512)S(1)}, s32[512]{0:T(512)}, u32[]{:S(2)}) copy-start(s32[512]{0:T(512)} %param.17) | copy-start | bytes 6148
  6.5 19.1 %copy-start.6 = (f32[64,6]{0,1:T(8,128)S(1)}, f32[64,6]{0,1:T(8,128)}, u32[]{:S(2)}) copy-start(f32[64,6]{0,1:T(8,128)} %param.20) | copy-start | bytes 4612
  6.5 34.5 %all-gather.2.cloned.1.call-start = ((), (), s32[]{:S(2)}) async-start(), calls=%async_computation.3 | async-start | bytes 1179648 | tf_op jit(solution)/shard_map/all_gather | solution.py:322
  22.1 8.8 %all-to-all-start.2 = ((bf16[4,16,2048]{2,1,0:T(8,128)(2,1)}), bf16[4,16,2048]{2,1,0:T(8,128)(2,1)S(1)}, u32[]{:S(2)}, u32[]{:S(2)}) async-start(bf16[4,16,2048]{2,1,0:T(8,128)(2,1)} %get-tuple-element.49), calls=%async_computation.2 | async-start | bytes 524288 | tf_op jit(solution)/shard_map/all_to_all | solution.py:304
  30.9 8.8 %all-to-all-start = ((bf16[4,16,2048]{2,1,0:T(8,128)(2,1)}), bf16[4,16,2048]{2,1,0:T(8,128)(2,1)S(1)}, u32[]{:S(2)}, u32[]{:S(2)}) async-start(bf16[4,16,2048]{2,1,0:T(8,128)(2,1)} %get-tuple-element.48), calls=%async_computation | async-start | bytes 524288 | tf_op jit(solution)/shard_map/all_to_all | solution.py:303
  46.7 2.8 %copy-start.4 = (f32[2048]{0:T(1024)S(1)}, f32[2048]{0:T(1024)}, u32[]{:S(2)}) copy-start(f32[2048]{0:T(1024)} %param.21) | copy-start | bytes 24580
  100.0 3.2 %copy-start.2 = (bf16[2,2,4,2,64,2048]{5,4,3,2,1,0:T(8,128)(2,1)}, bf16[2,2,4,2,64,2048]{5,4,3,2,1,0:T(8,128)(2,1)S(1)}, u32[]{:S(2)}) copy-start(bf16[2,2,4,2,64,2048]{5,4,3,2,1,0:T(8,128)(2,1)S(1)} %get-tuple-element.27) | copy-start | bytes 25165828
  117.6 3.0 %copy-start.3 = (bf16[4,8,56,2048]{3,2,1,0:T(8,128)(2,1)}, bf16[4,8,56,2048]{3,2,1,0:T(8,128)(2,1)S(1)}, u32[]{:S(2)}) copy-start(bf16[4,8,56,2048]{3,2,1,0:T(8,128)(2,1)S(1)} %copy.94) | copy-start | bytes 22020100
  151.5 62.6 %slice-start = ((s8[5767168]{0:T(1024)(128)(4,1)}), s8[4194304]{0:T(1024)(128)(4,1)S(1)}, s32[]{:S(2)}) async-start(s8[5767168]{0:T(1024)(128)(4,1)} %bitcast.134), calls=%async_computation.4 | async-start | bytes 8388608
  207.5 6.5 %slice-start.1 = ((s8[5767168]{0:T(1024)(128)(4,1)}), s8[1572864]{0:T(1024)(128)(4,1)S(1)}, s32[]{:S(2)}) async-start(s8[5767168]{0:T(1024)(128)(4,1)} %bitcast.134), calls=%async_computation.5 | async-start | bytes 3145728
  214.1 1.9 copy-start.1
Sparse Core Ops, SparseCore 0:
  19.2 21.8 all-gather.1

commit v3 on v2

--- a/solution.py
+++ b/solution.py
@@ -257,7 +257,7 @@
     rank = jnp.einsum(
         "ut,dtj->duj", before, named.astype(jnp.bfloat16), preferred_element_type=jnp.float32
     ).astype(jnp.int32)
-    joined = 4
+    joined = 8
     blocks = devices // joined
     place = jnp.arange(devices, dtype=jnp.int32)[:, None, None] % joined * CAP + rank
     place = jnp.where(named, place, -1).reshape(blocks, joined * token_rows, local_experts)

time: 223 us -> 225 us (level)
    unnamed x22 -> x17, local copies, waits for them, and re-layouts: 6.36 us -> 6.34 us
  transfers between devices with their start and end apart: 3 -> 3, of which waited for: 3 -> 3; matrix products, arithmetic and copies ran while one was open for 2% -> 3% of each run, Pallas kernels for 0% -> 0%
where the time goes in v3:
time: 225 us
  Pallas kernels  106 us (47%)
  matrix products  53.6 us (24%)
  local copies, waits for them, and re-layouts  20.7 us (9%)
  between operations  13.7 us (6%)
  blocking collectives  10.1 us (4%)
  waiting for transfers between devices  8.46 us (4%)
  starting transfers between devices  6.81 us (3%)
  other arithmetic  4.9 us (2%)
    pallas_call x1, Pallas kernels, scatter_sum(): pl.pallas_call(functools.partial(scatter_kernel, zs), out_shape=jax.Shape...  55.9 us
    pallas_call x1, Pallas kernels, gather_all(): pl.pallas_call(functools.partial(gather_kernel, zs), out_shape=(jax.Shape...  50.4 us
    dot_general x1, matrix products, body(): jnp.einsum('jsf,jfd->jsd', hidden, expert_down, preferred_element_type=jn...  14.1 us
    all_to_all x1, blocking collectives, body(): lax.all_to_all(by_dest(keys_values), 'req', split_axis=0, concat_axis=0,...  10.1 us
    dot_general x1, matrix products, body(): jnp.einsum('bjst,jbsd->btd', placing, down_out.reshape(local_experts, blo...  9.85 us
    dot_general x1, matrix products, body(): jnp.einsum('bjst,btd->jbsd', placing, all_rows.reshape(blocks, block_rows...  9.35 us
    dot_general x1, matrix products, body(): jnp.einsum('jsd,jfd->jsf', slot_rows, expert_gate_up[:, 0], preferred_ele...  8.08 us
    dot_general x1, matrix products, body(): jnp.einsum('td,dcf->tcf', normed, shared_gate_up, preferred_element_type=...  6.5 us
  transfers between devices with their start and end apart: 3, of which 3 were waited for; matrix products, arithmetic and copies ran while one was open for 3% of the time, Pallas kernels for 0%

profile of v3, /device:TPU:0, one launch (start us, length us, event | category | flops | bytes accessed | tf_op | source)
XLA Modules:
  0.0 224.7 jit_solution(12910381428254387996)
XLA Ops:
  6.5 0.0 copy-start
  6.5 0.0 copy-start.5
  6.5 0.0 all-gather.2.cloned.1.call-start
  6.5 0.8 select_reduce_fusion.1
  7.4 1.5 gather_fusion
  8.9 0.1 broadcast_select_fusion.2
  8.9 10.1 %all_to_all.15 = bf16[4,16,1024]{2,1,0:T(8,128)(2,1)} all-to-all(bf16[4,16,1024]{2,1,0:T(8,128)(2,1)S(1)} %broadcast_select_fusion.2), channel_id=1, replica_groups=mesh['req'=4,'head'=8] {'req'}, dimensions={0} | all-to-all | bytes 262144 | tf_op jit(solution)/shard_map/all_to_all | solution.py:305
  19.0 0.0 all-gather.2.cloned.1.call-update
  19.1 0.0 copy-done
  19.1 0.6 gather_fusion.1
  19.7 1.5 gather_fusion.2
  21.2 0.9 broadcast_select_fusion.1
  22.1 3.4 %all-to-all-start.2 = ((bf16[4,16,2048]{2,1,0:T(8,128)(2,1)}), bf16[4,16,2048]{2,1,0:T(8,128)(2,1)S(1)}, u32[]{:S(2)}, u32[]{:S(2)}) async-start(bf16[4,16,2048]{2,1,0:T(8,128)(2,1)} %get-tuple-element.49), calls=%async_computation.2 | async-start | bytes 524288 | tf_op jit(solution)/shard_map/all_to_all | solution.py:304
  25.5 0.7 convert_element_type.62
  26.2 0.8 dynamic_slice.7
  27.0 0.7 maximum_bitcast_fusion
  27.7 3.1 %all-to-all-done.2 = bf16[4,16,2048]{2,1,0:T(8,128)(2,1)S(1)} async-done(((bf16[4,16,2048]{2,1,0:T(8,128)(2,1)}), bf16[4,16,2048]{2,1,0:T(8,128)(2,1)S(1)}, u32[]{:S(2)}, u32[]{:S(2)}) %all-to-all-start.2) | async-done | bytes 262176 | tf_op jit(solution)/shard_map/all_to_all | solution.py:304
  30.8 3.4 %all-to-all-start = ((bf16[4,16,2048]{2,1,0:T(8,128)(2,1)}), bf16[4,16,2048]{2,1,0:T(8,128)(2,1)S(1)}, u32[]{:S(2)}, u32[]{:S(2)}) async-start(bf16[4,16,2048]{2,1,0:T(8,128)(2,1)} %get-tuple-element.48), calls=%async_computation | async-start | bytes 524288 | tf_op jit(solution)/shard_map/all_to_all | solution.py:303
  34.2 0.0 copy-done.5
  34.3 0.1 fusion.45
  34.4 0.2 reshape_reshape.3
  34.5 5.1 %all-to-all-done = bf16[4,16,2048]{2,1,0:T(8,128)(2,1)S(1)} async-done(((bf16[4,16,2048]{2,1,0:T(8,128)(2,1)}), bf16[4,16,2048]{2,1,0:T(8,128)(2,1)S(1)}, u32[]{:S(2)}, u32[]{:S(2)}) %all-to-all-start) | async-done | bytes 262176 | tf_op jit(solution)/shard_map/all_to_all | solution.py:303
  39.6 1.2 reshape.151
  40.8 0.3 all-gather.2.cloned.1.call-done
  41.0 1.3 fusion.61
  42.3 1.0 copy.80
  43.3 1.6 fusion.14
  44.9 0.7 fusion.21
  45.6 1.0 copy.83
  46.6 0.0 copy-start.4
  46.6 2.1 fusion.36
  48.8 0.3 copy.85
  49.1 0.2 reshape.140
  49.4 0.0 copy-done.4
  49.4 0.1 multiply_convert_fusion.1
  49.5 50.4 %shard_map.118 = (bf16[2,2,4,2,64,2048]{5,4,3,2,1,0:T(8,128)(2,1)S(1)}, f32[2,2,4,2,16,128]{5,4,3,2,1,0:T(8,128)S(1)}) custom-call(bf16[64,2048]{1,0:T(8,128)(2,1)S(1)} %get-tuple-element.28.n_ref, f32[16,128]{1,0:T(8,128)S(1)} %pad.4.m_ref), custom_call_target="tpu_custom_call" | custom-call | tf_op jit(solution)/shard_map/pallas_call | solution.py:126
  100.0 0.0 copy-start.2
  100.0 3.2 %copy-done.2 = bf16[2,2,4,2,64,2048]{5,4,3,2,1,0:T(8,128)(2,1)} copy-done((bf16[2,2,4,2,64,2048]{5,4,3,2,1,0:T(8,128)(2,1)}, bf16[2,2,4,2,64,2048]{5,4,3,2,1,0:T(8,128)(2,1)S(1)}, u32[]{:S(2)}) %copy-start.2) | copy-done | bytes 8388632
  103.2 0.1 copy.122
  103.3 0.1 reshape.142
  103.4 0.1 compare_reduce_fusion
  103.5 0.1 fusion.42
  103.7 0.1 reshape.143
  103.8 0.2 fusion.29
  104.0 0.1 reshape.144
  104.1 0.5 select_reduce_fusion
  104.6 0.1 mul.112
  104.7 9.4 %convert_bitcast_fusion = bf16[4,4,112,2048]{3,2,0,1:T(8,128)(2,1)} fusion(bf16[4,512,2048,1]{2,1,3,0:T(8,128)(2,1)} %bitcast.124, s32[4,4,512]{2,1,0:T(4,128)S(1)} %copy.89), kind=kOutput, calls=%fused_computation.8 | convolution fusion | flops 3762683904 | bytes 15761408 | tf_op jit(solution)/shard_map/bjst,btd->jbsd/dot_general | solution.py:396
  114.0 4.5 %copy.90 = bf16[4,4,112,2048]{3,2,1,0:T(8,128)(2,1)S(1)} copy(bf16[4,4,112,2048]{3,2,0,1:T(8,128)(2,1)} %convert_bitcast_fusion) | data formatting | bytes 14680064 | tf_op jit(solution)/shard_map/convert_element_type | solution.py:401
  118.5 0.0 copy-start.3
  118.5 3.0 %copy-done.3 = bf16[4,4,112,2048]{3,2,1,0:T(8,128)(2,1)} copy-done((bf16[4,4,112,2048]{3,2,1,0:T(8,128)(2,1)}, bf16[4,4,112,2048]{3,2,1,0:T(8,128)(2,1)S(1)}, u32[]{:S(2)}) %copy-start.3) | copy-done | bytes 7340056
  121.5 8.1 %fusion.6 = f32[4,448,352]{2,1,0:T(8,128)} fusion(bf16[4,448,2048]{2,1,0:T(8,128)(2,1)S(1)} %bitcast.126, bf16[4,2,352,2048]{3,2,1,0:T(8,128)(2,1)} %param.24), kind=kOutput, calls=%fused_computation.11 | convolution fusion | flops 2583691264 | bytes 15630336 | tf_op jit(solution)/shard_map/jsd,jfd->jsf/dot_general | solution.py:403
  129.6 14.1 %convolution_convert_fusion = bf16[4,448,2048]{2,1,0:T(8,128)(2,1)} fusion(bf16[4,352,2048]{2,1,0:T(8,128)(2,1)} %param.25, f32[4,448,352]{2,1,0:T(8,128)} %fusion.6, bf16[4,448,2048]{2,1,0:T(8,128)(2,1)} %bitcast.127, bf16[4,2,352,2048]{3,2,1,0:T(8,128)(2,1)} %param.24, f32[4,448]{1,0:T(4,128)S(1)} %mul.112), kind=kOutput, calls=%fused_computation.15 | convolution fusion | flops 5174837248 | bytes 28974080 | tf_op jit(solution)/shard_map/jsf,jfd->jsd/dot_general | solution.py:410
  143.6 9.8 %bitcast_convert_fusion = bf16[4,512,2048]{2,1,0:T(8,128)(2,1)} fusion(bf16[4,4,112,2048]{3,2,1,0:T(8,128)(2,1)} %bitcast.140, s32[4,4,512]{2,1,0:T(4,128)S(1)} %copy.89), kind=kOutput, calls=%fused_computation.3 | convolution fusion | flops 3763208192 | bytes 15761408 | tf_op jit(solution)/shard_map/bjst,jbsd->btd/dot_general | solution.py:413
  153.5 0.0 slice-start
  153.5 55.9 %shard_map.119 = f32[64,2048]{1,0:T(8,128)S(1)} custom-call(bf16[2,2,4,2,64,2048]{5,4,3,2,1,0:T(8,128)(2,1)} %bitcast.125), custom_call_target="tpu_custom_call" | custom-call | tf_op jit(solution)/shard_map/pallas_call | solution.py:229
  209.4 0.0 slice-start.1
  209.5 6.5 %fusion = f32[64,2,1408]{2,0,1:T(8,128)S(1)} fusion(bf16[2048,2,1408]{2,1,0:T(2,128)(2,1)} %param.22, bf16[64,2048]{1,0:T(8,128)(2,1)S(1)} %get-tuple-element.28.n_ref), kind=kOutput, calls=%fused_computation.4 | convolution fusion | flops 738197504 | bytes 12517376 | tf_op jit(solution)/shard_map/td,dcf->tcf/dot_general | solution.py:369
  216.0 0.0 copy-start.1
  216.0 0.0 slice-done
  216.0 0.0 slice-done.1
  216.0 1.8 fusion.13
  217.8 0.0 copy-done.1
  (17 shorter events, 0.1 us)
Async XLA Ops:
  6.5 12.6 %copy-start = (bf16[64,2048]{1,0:T(8,128)(2,1)S(1)}, bf16[64,2048]{1,0:T(8,128)(2,1)}, u32[]{:S(2)}) copy-start(bf16[64,2048]{1,0:T(8,128)(2,1)} %param.14) | copy-start | bytes 786436
  6.5 27.7 %copy-start.5 = (s32[512]{0:T(512)S(1)}, s32[512]{0:T(512)}, u32[]{:S(2)}) copy-start(s32[512]{0:T(512)} %param.17) | copy-start | bytes 6148
  6.5 34.5 %all-gather.2.cloned.1.call-start = ((), (), s32[]{:S(2)}) async-start(), calls=%async_computation.3 | async-start | bytes 1179648 | tf_op jit(solution)/shard_map/all_gather | solution.py:322
  22.1 8.8 %all-to-all-start.2 = ((bf16[4,16,2048]{2,1,0:T(8,128)(2,1)}), bf16[4,16,2048]{2,1,0:T(8,128)(2,1)S(1)}, u32[]{:S(2)}, u32[]{:S(2)}) async-start(bf16[4,16,2048]{2,1,0:T(8,128)(2,1)} %get-tuple-element.49), calls=%async_computation.2 | async-start | bytes 524288 | tf_op jit(solution)/shard_map/all_to_all | solution.py:304
  30.8 8.8 %all-to-all-start = ((bf16[4,16,2048]{2,1,0:T(8,128)(2,1)}), bf16[4,16,2048]{2,1,0:T(8,128)(2,1)S(1)}, u32[]{:S(2)}, u32[]{:S(2)}) async-start(bf16[4,16,2048]{2,1,0:T(8,128)(2,1)} %get-tuple-element.48), calls=%async_computation | async-start | bytes 524288 | tf_op jit(solution)/shard_map/all_to_all | solution.py:303
  46.6 2.7 %copy-start.4 = (f32[2048]{0:T(1024)S(1)}, f32[2048]{0:T(1024)}, u32[]{:S(2)}) copy-start(f32[2048]{0:T(1024)} %param.21) | copy-start | bytes 24580
  100.0 3.2 %copy-start.2 = (bf16[2,2,4,2,64,2048]{5,4,3,2,1,0:T(8,128)(2,1)}, bf16[2,2,4,2,64,2048]{5,4,3,2,1,0:T(8,128)(2,1)S(1)}, u32[]{:S(2)}) copy-start(bf16[2,2,4,2,64,2048]{5,4,3,2,1,0:T(8,128)(2,1)S(1)} %get-tuple-element.27) | copy-start | bytes 25165828
  118.5 3.0 %copy-start.3 = (bf16[4,4,112,2048]{3,2,1,0:T(8,128)(2,1)}, bf16[4,4,112,2048]{3,2,1,0:T(8,128)(2,1)S(1)}, u32[]{:S(2)}) copy-start(bf16[4,4,112,2048]{3,2,1,0:T(8,128)(2,1)S(1)} %copy.90) | copy-start | bytes 22020100
  153.5 62.5 %slice-start = ((s8[5767168]{0:T(1024)(128)(4,1)}), s8[4194304]{0:T(1024)(128)(4,1)S(1)}, s32[]{:S(2)}) async-start(s8[5767168]{0:T(1024)(128)(4,1)} %bitcast.128), calls=%async_computation.4 | async-start | bytes 8388608
  209.4 6.5 %slice-start.1 = ((s8[5767168]{0:T(1024)(128)(4,1)}), s8[1572864]{0:T(1024)(128)(4,1)S(1)}, s32[]{:S(2)}) async-start(s8[5767168]{0:T(1024)(128)(4,1)} %bitcast.128), calls=%async_computation.5 | async-start | bytes 3145728
  216.0 1.9 copy-start.1
Sparse Core Ops, SparseCore 0:
  19.2 21.8 all-gather.1
